TPU v7x, 32 devices: a whole 2x2x4 slice. The times are simulated.
32 devices in a mesh: dp: 16 (over z, y, x), tensor: 2 (over core).
Axes of the slice: x: 2, y: 2, z: 4, core: 2. Of those that a mesh axis runs over, the one named last changes fastest.
Arguments:
- tokens: bfloat16 [16384, 768], P(('dp', 'tensor')), may hold values from -6 to 6
- lengths: int32 [16], P('dp'), may hold values from 1 to 1024, 10240 in all
- qkv_weight: bfloat16 [3, 768, 768], P(None, 'dp', 'tensor'), may hold values from -0.21875 to 0.21875
- qv_bias: float32 [2, 768], P(None, 'tensor'), may hold values from -3 to 3
- out_weight: bfloat16 [768, 768], P('tensor', 'dp'), may hold values from -0.875 to 0.875
- out_bias: float32 [768], replicated, may hold values from -3 to 3
- up_weight: bfloat16 [768, 3072], P('dp', 'tensor'), may hold values from -0.21875 to 0.21875
- up_bias: float32 [3072], P('tensor'), may hold values from -3 to 3
- down_weight: bfloat16 [3072, 768], P('tensor', 'dp'), may hold values from -0.109375 to 0.109375
- down_bias: float32 [768], replicated, may hold values from -3 to 3
- norm1_gain: float32 [768], replicated, may hold values from 0.5 to 1.5
- norm1_shift: float32 [768], replicated, may hold values from -3 to 3
- norm2_gain: float32 [768], replicated, may hold values from 0.5 to 1.5
- norm2_shift: float32 [768], replicated, may hold values from -3 to 3
- cotangent: bfloat16 [16384, 768], P(('dp', 'tensor')), may hold values from -6 to 6
Outputs:
- layer_output: bfloat16 [16384, 768], P(('dp', 'tensor'))
- input_grad: bfloat16 [16384, 768], P(('dp', 'tensor'))
- grad_qkv_weight: float32 [3, 768, 768], P(None, 'dp', 'tensor')
- grad_qv_bias: float32 [2, 768], P(None, 'tensor')
- grad_out_weight: float32 [768, 768], P('tensor', 'dp')
- grad_out_bias: float32 [768], replicated
- grad_up_weight: float32 [768, 3072], P('dp', 'tensor')
- grad_up_bias: float32 [3072], P('tensor')
- grad_down_weight: float32 [3072, 768], P('tensor', 'dp')
- grad_down_bias: float32 [768], replicated
- grad_norm1_gain: float32 [768], replicated
- grad_norm1_shift: float32 [768], replicated
- grad_norm2_gain: float32 [768], replicated
- grad_norm2_shift: float32 [768], replicated
Inputs may be any that keep to these rules, and one draw needn't show every extreme that they name: lengths[s] is the count of real tokens of sequence s; some sequence has 1024.
All inputs are finite; a program needn't handle non-finite values. No bound on the sum of `lengths` on one device may be relied on, other than what follows from the above.
Results may differ from a plain program's by a relative error of at most 0.017.
Values may be sent and summed in bfloat16 or wider, within the bound.
A program may use at most 192 MiB of HBM per device.

v0:
```python
import jax
import jax.numpy as jnp
from jax import lax
from jax.sharding import PartitionSpec as P

HEAD_DIM = 64
LENGTH = 1024
EPSILON = 1e-05
NEGATIVE = -1e30


def layer_norm(values, norm_gain, norm_shift):
    center = values - jnp.mean(values, axis=-1, keepdims=True)
    spread = jnp.mean(center * center, axis=-1, keepdims=True)
    return center * lax.rsqrt(spread + EPSILON) * norm_gain + norm_shift


def gelu_exact(values):
    return jax.nn.gelu(values, approximate=False)


def matmul(left, right):
    return jnp.dot(left, right, preferred_element_type=jnp.float32)


def contract_rows(left, right):
    return lax.dot_general(
        left, right, (((0,), (0,)), ((), ())), preferred_element_type=jnp.float32
    )


def contract_cols(left, right):
    return lax.dot_general(
        left, right, (((1,), (1,)), ((), ())), preferred_element_type=jnp.float32
    )


def per_device(
    tokens,
    lengths,
    qkv_weight,
    qv_bias,
    out_weight,
    out_bias,
    up_weight,
    up_bias,
    down_weight,
    down_bias,
    norm1_gain,
    norm1_shift,
    norm2_gain,
    norm2_shift,
    cotangent,
):
    tok_rows = tokens.shape[0]
    local_width = qkv_weight.shape[2]
    head_count = local_width // HEAD_DIM
    seq_count = lengths.shape[0]
    block_rows = min(512, LENGTH)
    scaling = HEAD_DIM ** (-0.5)
    positions = jnp.arange(LENGTH)
    qkv_full, out_full, up_full, down_full = (
        lax.all_gather(qkv_weight, "dp", axis=1, tiled=True),
        lax.all_gather(out_weight, "dp", axis=1, tiled=True),
        lax.all_gather(up_weight, "dp", axis=0, tiled=True),
        lax.all_gather(down_weight, "dp", axis=1, tiled=True),
    )
    gathered = lax.all_gather(tokens, "tensor", axis=0, tiled=True)
    queries = (matmul(gathered, qkv_full[0]) + qv_bias[0]).astype(jnp.bfloat16)
    key_rows = matmul(gathered, qkv_full[1]).astype(jnp.bfloat16)
    value_rows = (matmul(gathered, qkv_full[2]) + qv_bias[1]).astype(jnp.bfloat16)

    def forward_seq(packed):
        seq_queries, seq_keys, seq_values, length = packed
        query_heads = seq_queries.reshape(LENGTH, head_count, HEAD_DIM)
        key_heads = seq_keys.reshape(LENGTH, head_count, HEAD_DIM)
        value_heads = seq_values.reshape(LENGTH, head_count, HEAD_DIM)
        usable = (positions < length)[None, None, :]
        context_blocks = []
        total_blocks = []
        for block_start in range(0, LENGTH, block_rows):
            block_q = query_heads[block_start : block_start + block_rows]
            scores = (
                jnp.einsum("qhd,khd->hqk", block_q, key_heads, preferred_element_type=jnp.float32)
                * scaling
            )
            scores = jnp.where(usable, scores, NEGATIVE)
            row_top = jnp.max(scores, axis=-1, keepdims=True)
            exponent = jnp.exp(scores - row_top)
            row_total = jnp.sum(exponent, axis=-1, keepdims=True)
            weights = (exponent / row_total).astype(jnp.bfloat16)
            block_context = jnp.einsum(
                "hqk,khd->qhd", weights, value_heads, preferred_element_type=jnp.float32
            )
            context_blocks.append(block_context.reshape(block_rows, local_width))
            total_blocks.append((row_top + jnp.log(row_total))[..., 0])
        return (
            jnp.concatenate(context_blocks, axis=0).astype(jnp.bfloat16),
            jnp.concatenate(total_blocks, axis=1),
        )

    shaped = (
        queries.reshape(seq_count, LENGTH, local_width),
        key_rows.reshape(seq_count, LENGTH, local_width),
        value_rows.reshape(seq_count, LENGTH, local_width),
    )
    contexts, log_totals = lax.map(forward_seq, (shaped[0], shaped[1], shaped[2], lengths))
    context_flat = contexts.reshape(seq_count * LENGTH, local_width)
    row_block = lax.slice_in_dim(context_flat, 0, tok_rows * lax.axis_size("tensor"), axis=0)
    attn = (
        lax.psum_scatter(matmul(row_block, out_full), "tensor", scatter_dimension=0, tiled=True)
        + out_bias
    )
    first_sum = tokens.astype(jnp.float32) + attn
    hidden = layer_norm(first_sum, norm1_gain, norm1_shift)
    hidden_low = hidden.astype(jnp.bfloat16)
    hidden_all = lax.all_gather(hidden_low, "tensor", axis=0, tiled=True)
    upper = matmul(hidden_all, up_full) + up_bias
    active = gelu_exact(upper).astype(jnp.bfloat16)
    row_block = lax.slice_in_dim(active, 0, tok_rows * lax.axis_size("tensor"), axis=0)
    ffn_out = (
        lax.psum_scatter(matmul(row_block, down_full), "tensor", scatter_dimension=0, tiled=True)
        + down_bias
    )
    second_sum = hidden + ffn_out
    layer_output = layer_norm(second_sum, norm2_gain, norm2_shift).astype(jnp.bfloat16)
    qkv_back, out_back, up_back, down_back = (qkv_full, out_full, up_full, down_full)
    unused_two, norm_two_back = jax.vjp(layer_norm, second_sum, norm2_gain, norm2_shift)
    grad_second, gain_two_grad, shift_two_grad = norm_two_back(cotangent.astype(jnp.float32))
    grad_ffn = grad_second.astype(jnp.bfloat16)
    down_bias_grad = jnp.sum(grad_ffn.astype(jnp.float32), axis=0)
    grad_ffn_all = lax.all_gather(grad_ffn, "tensor", axis=0, tiled=True)
    down_weight_grad = contract_rows(active, grad_ffn_all)
    grad_active = contract_cols(grad_ffn_all, down_back)
    unused_gelu, gelu_back = jax.vjp(gelu_exact, upper)
    grad_upper = gelu_back(grad_active)[0].astype(jnp.bfloat16)
    up_bias_grad = jnp.sum(grad_upper.astype(jnp.float32), axis=0)
    up_weight_grad = contract_rows(hidden_all, grad_upper)
    row_block = lax.slice_in_dim(grad_upper, 0, tok_rows * lax.axis_size("tensor"), axis=0)
    grad_hidden = grad_second + lax.psum_scatter(
        contract_cols(row_block, up_back), "tensor", scatter_dimension=0, tiled=True
    )
    unused_one, norm_one_back = jax.vjp(layer_norm, first_sum, norm1_gain, norm1_shift)
    grad_first, gain_one_grad, shift_one_grad = norm_one_back(grad_hidden)
    grad_attn = grad_first.astype(jnp.bfloat16)
    out_bias_grad = jnp.sum(grad_attn.astype(jnp.float32), axis=0)
    grad_attn_all = lax.all_gather(grad_attn, "tensor", axis=0, tiled=True)
    out_weight_grad = contract_rows(context_flat, grad_attn_all)
    grad_context = contract_cols(grad_attn_all, out_back).astype(jnp.bfloat16)

    def backward_seq(packed):
        seq_queries, seq_keys, seq_values, length, seq_grad, seq_totals = packed
        query_heads = seq_queries.reshape(LENGTH, head_count, HEAD_DIM)
        key_heads = seq_keys.reshape(LENGTH, head_count, HEAD_DIM)
        value_heads = seq_values.reshape(LENGTH, head_count, HEAD_DIM)
        usable = (positions < length)[None, None, :]
        key_grad = jnp.zeros((LENGTH, head_count, HEAD_DIM), jnp.float32)
        value_grad = jnp.zeros((LENGTH, head_count, HEAD_DIM), jnp.float32)
        query_blocks = []
        for block_start in range(0, LENGTH, block_rows):
            block_q = query_heads[block_start : block_start + block_rows]
            block_grad = seq_grad[block_start : block_start + block_rows].reshape(
                block_rows, head_count, HEAD_DIM
            )
            scores = (
                jnp.einsum("qhd,khd->hqk", block_q, key_heads, preferred_element_type=jnp.float32)
                * scaling
            )
            scores = jnp.where(usable, scores, NEGATIVE)
            chances = jnp.exp(scores - seq_totals[:, block_start : block_start + block_rows, None])
            weights = chances.astype(jnp.bfloat16)
            value_grad = value_grad + jnp.einsum(
                "hqk,qhd->khd", weights, block_grad, preferred_element_type=jnp.float32
            )
            grad_weights = jnp.einsum(
                "qhd,khd->hqk", block_grad, value_heads, preferred_element_type=jnp.float32
            )
            inner_sum = jnp.sum(grad_weights * chances, axis=-1, keepdims=True)
            grad_scores = (chances * (grad_weights - inner_sum)).astype(jnp.bfloat16)
            block_query_grad = (
                jnp.einsum(
                    "hqk,khd->qhd", grad_scores, key_heads, preferred_element_type=jnp.float32
                )
                * scaling
            )
            query_blocks.append(block_query_grad.reshape(block_rows, local_width))
            key_grad = (
                key_grad
                + jnp.einsum(
                    "hqk,qhd->khd", grad_scores, block_q, preferred_element_type=jnp.float32
                )
                * scaling
            )
        query_grad = jnp.concatenate(query_blocks, axis=0).astype(jnp.bfloat16)
        return (
            query_grad,
            key_grad.reshape(LENGTH, local_width).astype(jnp.bfloat16),
            value_grad.reshape(LENGTH, local_width).astype(jnp.bfloat16),
        )

    grad_shaped = grad_context.reshape(seq_count, LENGTH, local_width)
    query_grads, key_grads, value_grads = lax.map(
        backward_seq, (shaped[0], shaped[1], shaped[2], lengths, grad_shaped, log_totals)
    )
    query_grads = query_grads.reshape(seq_count * LENGTH, local_width)
    key_grads = key_grads.reshape(seq_count * LENGTH, local_width)
    value_grads = value_grads.reshape(seq_count * LENGTH, local_width)
    qv_bias_grad = jnp.stack(
        [
            jnp.sum(query_grads.astype(jnp.float32), axis=0),
            jnp.sum(value_grads.astype(jnp.float32), axis=0),
        ]
    )
    qkv_weight_grad = jnp.stack(
        [
            contract_rows(gathered, query_grads),
            contract_rows(gathered, key_grads),
            contract_rows(gathered, value_grads),
        ]
    )
    part_query = lax.slice_in_dim(query_grads, 0, lax.axis_size("tensor") * tok_rows, axis=0)
    input_grad = (
        grad_first
        + lax.psum_scatter(
            (
                contract_cols(part_query, qkv_back[0])
                + contract_cols(key_grads, qkv_back[1])
                + contract_cols(value_grads, qkv_back[2])
            ).astype(jnp.bfloat16),
            "tensor",
            scatter_dimension=0,
            tiled=True,
        ).astype(jnp.float32)
    ).astype(jnp.bfloat16)
    qkv_grad_own, out_grad_own, up_grad_own, down_grad_own = (
        lax.psum_scatter(qkv_weight_grad, "dp", scatter_dimension=1, tiled=True),
        lax.psum_scatter(out_weight_grad, "dp", scatter_dimension=1, tiled=True),
        lax.psum_scatter(up_weight_grad, "dp", scatter_dimension=0, tiled=True),
        lax.psum_scatter(down_weight_grad, "dp", scatter_dimension=1, tiled=True),
    )
    qv_bias_total, up_bias_total = lax.psum((qv_bias_grad, up_bias_grad), "dp")
    (
        out_bias_total,
        down_bias_total,
        gain_one_total,
        shift_one_total,
        gain_two_total,
        shift_two_total,
    ) = lax.psum(
        (
            out_bias_grad,
            down_bias_grad,
            gain_one_grad,
            shift_one_grad,
            gain_two_grad,
            shift_two_grad,
        ),
        ("dp", "tensor"),
    )
    return (
        layer_output,
        input_grad,
        qkv_grad_own,
        qv_bias_total,
        out_grad_own,
        out_bias_total,
        up_grad_own,
        up_bias_total,
        down_grad_own,
        down_bias_total,
        gain_one_total,
        shift_one_total,
        gain_two_total,
        shift_two_total,
    )


def solution(mesh):
    return jax.shard_map(
        per_device,
        mesh=mesh,
        in_specs=(
            P(("dp", "tensor"), None),
            P("dp"),
            P(None, "dp", "tensor"),
            P(None, "tensor"),
            P("tensor", "dp"),
            P(),
            P("dp", "tensor"),
            P("tensor"),
            P("tensor", "dp"),
            P(),
            P(),
            P(),
            P(),
            P(),
            P(("dp", "tensor"), None),
        ),
        out_specs=(
            P(("dp", "tensor"), None),
            P(("dp", "tensor"), None),
            P(None, "dp", "tensor"),
            P(None, "tensor"),
            P("tensor", "dp"),
            P(),
            P("dp", "tensor"),
            P("tensor"),
            P("tensor", "dp"),
            P(),
            P(),
            P(),
            P(),
            P(),
        ),
        check_vma=False,
    )
```

profile of v0, /device:TPU:0, one launch (start us, length us, event | category | flops | bytes accessed | tf_op | source)
XLA Modules:
  0.0 1038.2 jit_solution(9922317103957784277)
XLA Ops:
  10.1 49.1 %all_gather.26 = bf16[384,768]{0,1:T(8,128)(2,1)} all-gather(bf16[384,48]{0,1:T(8,128)(2,1)} %param.19), channel_id=1, replica_groups=mesh['dp'=16,'tensor'=2] {'dp'}, dimensions={1}, use_global_device_ids=true | all-gather | bytes 626688 | tf_op jit(solution)/shard_map/all_gather | solution.py:64
  59.2 25.9 %all-gather.10.cloned.1.call-done = bf16[3,768,384]{2,1,0:T(8,128)(2,1)} async-done(((bf16[3,48,384]{2,1,0:T(8,128)(2,1)}), bf16[3,768,384]{2,1,0:T(8,128)(2,1)}) %all-gather.10.cloned.1.call-update) | async-done | bytes 1769488 | tf_op jit(solution)/shard_map/all_gather | solution.py:63
  115.9 9.2 reduce-scatter.8.cloned.1.call-done
  129.2 62.5 %all-gather.14.cloned.1.call-done = bf16[768,1536]{1,0:T(8,128)(2,1)} async-done(((bf16[48,1536]{1,0:T(8,128)(2,1)}), bf16[768,1536]{1,0:T(8,128)(2,1)}) %all-gather.14.cloned.1.call-update) | async-done | bytes 2359312 | tf_op jit(solution)/shard_map/all_gather | solution.py:65
  191.6 10.7 %all-gather.12.cloned.1.call-done = bf16[1024,768]{1,0:T(8,128)(2,1)} async-done(((bf16[512,768]{1,0:T(8,128)(2,1)}), bf16[1024,768]{1,0:T(8,128)(2,1)}) %all-gather.12.cloned.1.call-update) | async-done | bytes 1572880 | tf_op jit(solution)/shard_map/all_gather | solution.py:117
  202.3 19.9 %multiply_convert_fusion.2 = (bf16[1024,1536]{1,0:T(8,128)(2,1)}, f32[1024,1536]{1,0:T(8,128)}, f32[1024,1536]{1,0:T(8,128)}) fusion(f32[1536]{0:T(1024)S(1)} %copy-done.44, bf16[1024,768]{1,0:T(8,128)(2,1)} %all-gather.12.cloned.1.call-done, bf16[768,1536]{1,0:T(8,128)(2,1)} %all-gather.14.cloned.1.call-done), kind=kOutput, calls=%fused_computation.24 | convolution fusion | flops 2519728128 | bytes 19666944 | tf_op jit(solution)/shard_map/dot_general | solution.py:23
  222.2 46.7 %all-gather.16.cloned.1.call-done = bf16[1536,768]{0,1:T(8,128)(2,1)} async-done(((bf16[1536,48]{0,1:T(8,128)(2,1)}), bf16[1536,768]{0,1:T(8,128)(2,1)}) %all-gather.16.cloned.1.call-update) | async-done | bytes 2359312 | tf_op jit(solution)/shard_map/all_gather | solution.py:66
  268.8 6.9 fusion.57
  275.8 9.8 reduce-scatter.10.cloned.1.call-done
  291.5 11.1 %all-gather.18.cloned.1.call-done = bf16[1024,768]{1,0:T(8,128)(2,1)} async-done(((bf16[512,768]{1,0:T(8,128)(2,1)}), bf16[1024,768]{1,0:T(8,128)(2,1)}) %all-gather.18.cloned.1.call-update) | async-done | bytes 1572880 | tf_op jit(solution)/shard_map/all_gather | solution.py:132
  302.5 10.9 %convert_reduce_fusion = (f32[1536]{0:T(1024)}, bf16[1024,1536]{1,0:T(8,128)(2,1)S(1)}) fusion(f32[1024,1536]{1,0:T(8,128)} %get-tuple-element.135, f32[1024,1536]{1,0:T(8,128)} %get-tuple-element.146, f32[1536]{0:T(1024)S(1)} %copy-done.44, bf16[1024,768]{1,0:T(8,128)(2,1)} %all-gather.18.cloned.1.call-done, ...), kind=kOutput, calls=%fused_computation.20 | convolution fusion | flops 2442656256 | bytes 19673088 | tf_op jit(solution)/shard_map/dot_general | solution.py:33
  319.5 12.2 %reduce-scatter.12.cloned.1.call-done = f32[512,768]{1,0:T(8,128)} async-done(((f32[1024,768]{1,0:T(8,128)}), f32[512,768]{1,0:T(8,128)}) %reduce-scatter.12.cloned.1.call-update) | async-done | bytes 1572880 | tf_op jit(solution)/shard_map/reduce_scatter | solution.py:140
  338.5 10.6 %all-gather.20.cloned.1.call-done = bf16[1024,768]{1,0:T(8,128)(2,1)} async-done(((bf16[512,768]{1,0:T(8,128)(2,1)}), bf16[1024,768]{1,0:T(8,128)(2,1)}) %all-gather.20.cloned.1.call-update) | async-done | bytes 1572880 | tf_op jit(solution)/shard_map/all_gather | solution.py:147
  351.4 6.4 fusion.59
  357.9 7.3 fusion.5
  365.1 18.9 %multiply_reduce_fusion.1 = (f32[6,512]{1,0:T(8,128)S(1)}, f32[6,512]{1,0:T(8,128)S(1)}, f32[6,512,1024]{2,1,0:T(8,128)}) fusion(f32[6,512]{1,0:T(8,128)S(1)} %get-tuple-element.151, f32[6,512,1024]{2,1,0:T(8,128)} %copy-done.1, pred[1024]{0:T(1024)(128)(4,1)S(1)} %iota_compare_fusion, f32[6,512,1024]{2,1,0:T(8,128)} %fusion.59, ...), kind=kOutput, calls=%fused_computation.4 | convolution fusion | flops 434104320 | bytes 51561472 | tf_op jit(solution)/shard_map/while/body/eval_jaxpr/qhd,khd->hqk/dot_general | solution.py:175
  384.1 17.3 %multiply_convert_fusion.1 = (bf16[6,512,1024]{2,1,0:T(8,128)(2,1)S(1)}, bf16[6,512,1024]{2,1,0:T(8,128)(2,1)S(1)}) fusion(f32[6,512,1024]{2,1,0:T(8,128)} %get-tuple-element.147, f32[6,512]{1,0:T(8,128)S(1)} %get-tuple-element.107, f32[6,512]{1,0:T(8,128)S(1)} %get-tuple-element.151, f32[6,512,1024]{2,1,0:T(8,128)} %copy-done.1, ...), kind=kLoop, calls=%fused_computation.3 | loop fusion | flops 37748736 | bytes 62964736 | tf_op jit(solution)/shard_map/while/body/eval_jaxpr/convert_element_type | solution.py:179
  405.0 7.2 convert_reduce_fusion.4
  449.8 43.9 %all-reduce.1 = (f32[768]{0:T(1024)}, f32[768]{0:T(1024)}, f32[768]{0:T(1024)}, f32[768]{0:T(1024)}, f32[768]{0:T(1024)}, /*index=5*/f32[768]{0:T(1024)}) all-reduce(f32[768]{0:T(1024)S(1)} %copy-done.30, f32[768]{0:T(1024)S(1)} %get-tuple-element.121, f32[768]{0:T(1024)S(1)} %copy-done.32, ...), channel_id=1, replica_groups=mesh['dp'=16,'tensor'=2] {'dp','tensor'}, use_global_device_ids=true, to_apply=%region_24.25 | all-reduce | flops 4608 | bytes 36864 | tf_op jit(solution)/shard_map/psum | solution.py:249
  494.0 76.4 %all-reduce.2 = (f32[2,384]{1,0:T(2,128)}, f32[1536]{0:T(1024)}) all-reduce(f32[2,384]{1,0:T(2,128)S(1)} %pad_maximum_fusion.7, f32[1536]{0:T(1024)S(1)} %copy-done.34), channel_id=1, replica_groups=mesh['dp'=16,'tensor'=2] {'dp'}, use_global_device_ids=true, to_apply=%region_21.22 | all-reduce | flops 2304 | bytes 18432 | tf_op jit(solution)/shard_map/psum | solution.py:241
  572.7 45.6 %all-reduce.5.cloned.1.call-done = f32[3,768,384]{2,0,1:T(4,128)} async-done(((f32[3,768,384]{2,0,1:T(4,128)}), f32[3,768,384]{2,0,1:T(4,128)}) %all-reduce.5.cloned.1.call-update) | async-done | bytes 3538960
  620.1 141.2 %reduce-scatter.20.cloned.1.call-done = f32[1536,48]{0,1:T(8,128)} async-done(((f32[1536,768]{0,1:T(8,128)}), f32[1536,48]{0,1:T(8,128)}) %reduce-scatter.20.cloned.1.call-update) | async-done | bytes 294928 | tf_op jit(solution)/shard_map/reduce_scatter | solution.py:239
  761.2 141.7 %reduce-scatter.18.cloned.1.call-done = f32[48,1536]{1,0:T(8,128)} async-done(((f32[768,1536]{1,0:T(8,128)}), f32[48,1536]{1,0:T(8,128)}) %reduce-scatter.18.cloned.1.call-update) | async-done | bytes 294928 | tf_op jit(solution)/shard_map/reduce_scatter | solution.py:238
  902.9 128.6 %reduce-scatter.16.cloned.1.call-done = f32[384,48]{0,1:T(8,128)} async-done(((f32[384,768]{0,1:T(8,128)}), f32[384,48]{0,1:T(8,128)}) %reduce-scatter.16.cloned.1.call-update) | async-done | bytes 73744 | tf_op jit(solution)/shard_map/reduce_scatter | solution.py:237
  (184 shorter events, 102.2 us)
Async XLA Ops:
  7.2 52.0 %all-gather.8.cloned.1.call-start = ((), (), s32[]{:S(2)}) async-start(), calls=%async_computation.7 | async-start | bytes 2359296 | tf_op jit(solution)/shard_map/all_gather | solution.py:68
  7.9 77.2 %all-gather.10.cloned.1.call-start = ((), (), s32[]{:S(2)}) async-start(), calls=%async_computation.8 | async-start | bytes 1880064 | tf_op jit(solution)/shard_map/all_gather | solution.py:63
  8.7 116.4 %reduce-scatter.8.cloned.1.call-start = ((), (), s32[]{:S(2)}) async-start(), calls=%async_computation.9 | async-start | bytes 4718592 | tf_op jit(solution)/shard_map/reduce_scatter | solution.py:111
  59.2 28.3 %copy-start.40 = (bf16[1024,768]{1,0:T(8,128)(2,1)S(1)}, bf16[1024,768]{1,0:T(8,128)(2,1)}, u32[]{:S(2)}) copy-start(bf16[1024,768]{1,0:T(8,128)(2,1)} %all-gather.8.cloned.1.call-done) | copy-start | bytes 4718596
  115.3 76.3 %all-gather.14.cloned.1.call-start = ((), (), s32[]{:S(2)}) async-start(), calls=%async_computation.11 | async-start | bytes 2506752 | tf_op jit(solution)/shard_map/all_gather | solution.py:65
  115.9 86.4 %all-gather.12.cloned.1.call-start = ((), (), s32[]{:S(2)}) async-start(), calls=%async_computation.10 | async-start | bytes 2359296 | tf_op jit(solution)/shard_map/all_gather | solution.py:117
  126.8 75.5 %copy-start.44 = (f32[1536]{0:T(1024)S(1)}, f32[1536]{0:T(1024)}, u32[]{:S(2)}) copy-start(f32[1536]{0:T(1024)} %param.22) | copy-start | bytes 18436
  128.4 140.5 %all-gather.16.cloned.1.call-start = ((), (), s32[]{:S(2)}) async-start(), calls=%async_computation.12 | async-start | bytes 2506752 | tf_op jit(solution)/shard_map/all_gather | solution.py:66
  128.9 156.7 %reduce-scatter.10.cloned.1.call-start = ((), (), s32[]{:S(2)}) async-start(), calls=%async_computation.13 | async-start | bytes 4718592 | tf_op jit(solution)/shard_map/reduce_scatter | solution.py:122
  275.8 26.8 %all-gather.18.cloned.1.call-start = ((), (), s32[]{:S(2)}) async-start(), calls=%async_computation.14 | async-start | bytes 2359296 | tf_op jit(solution)/shard_map/all_gather | solution.py:132
  291.4 40.3 %reduce-scatter.12.cloned.1.call-start = ((), (), s32[]{:S(2)}) async-start(), calls=%async_computation.15 | async-start | bytes 4718592 | tf_op jit(solution)/shard_map/reduce_scatter | solution.py:140
  319.5 29.7 %all-gather.20.cloned.1.call-start = ((), (), s32[]{:S(2)}) async-start(), calls=%async_computation.16 | async-start | bytes 2359296 | tf_op jit(solution)/shard_map/all_gather | solution.py:147
  338.0 232.5 %reduce-scatter.14.cloned.1.call-start = ((), (), s32[]{:S(2)}) async-start(), calls=%async_computation.17 | async-start | bytes 2359296 | tf_op jit(solution)/shard_map/reduce_scatter | solution.py:224
  384.1 17.3 %copy-start.5 = (bf16[1024,384]{0,1:T(8,128)(2,1)S(1)}, bf16[1024,384]{0,1:T(8,128)(2,1)}, u32[]{:S(2)}) copy-start(bf16[1024,384]{0,1:T(8,128)(2,1)} %copy-done.4) | copy-start | bytes 2359300
  403.5 16.7 %copy-start.10 = (bf16[6,64,512]{2,1,0:T(8,128)(2,1)}, bf16[6,64,512]{2,1,0:T(8,128)(2,1)S(1)}, u32[]{:S(2)}) copy-start(bf16[6,64,512]{2,1,0:T(8,128)(2,1)S(1)} %fusion.27) | copy-start | bytes 1179652
  420.2 198.2 %all-reduce.5.cloned.1.call-start = ((), (), s32[]{:S(2)}) async-start(), calls=%async_computation.21 | async-start | bytes 9437184
  428.4 332.8 %reduce-scatter.20.cloned.1.call-start = ((), (), s32[]{:S(2)}) async-start(), calls=%async_computation.20 | async-start | bytes 5013504 | tf_op jit(solution)/shard_map/reduce_scatter | solution.py:239
  436.2 466.7 %reduce-scatter.18.cloned.1.call-start = ((), (), s32[]{:S(2)}) async-start(), calls=%async_computation.19 | async-start | bytes 5013504 | tf_op jit(solution)/shard_map/reduce_scatter | solution.py:238
  443.9 49.8 %copy-start.36 = (f32[6,64]{1,0:T(8,128)S(1)}, f32[6,64]{1,0:T(8,128)}, u32[]{:S(2)}) copy-start(f32[6,64]{1,0:T(8,128)} %get-tuple-element.148) | copy-start | bytes 4612
  443.9 49.9 %copy-start.11 = (bf16[6,64,512]{2,1,0:T(8,128)(2,1)S(1)}, bf16[6,64,512]{2,1,0:T(8,128)(2,1)}, u32[]{:S(2)}) copy-start(bf16[6,64,512]{2,1,0:T(8,128)(2,1)} %copy-done.10) | copy-start | bytes 1179652
  444.0 49.8 %copy-start.13 = (bf16[6,64,512]{2,1,0:T(8,128)(2,1)S(1)}, bf16[6,64,512]{2,1,0:T(8,128)(2,1)}, u32[]{:S(2)}) copy-start(bf16[6,64,512]{2,1,0:T(8,128)(2,1)} %copy-done.12) | copy-start | bytes 1179652
  444.0 50.0 %copy-start.34 = (f32[1536]{0:T(1024)S(1)}, f32[1536]{0:T(1024)}, u32[]{:S(2)}) copy-start(f32[1536]{0:T(1024)} %get-tuple-element.125) | copy-start | bytes 18436
  444.0 126.5 %copy-start.3 = (f32[512,768]{1,0:T(8,128)S(1)}, f32[512,768]{1,0:T(8,128)}, u32[]{:S(2)}) copy-start(f32[512,768]{1,0:T(8,128)} %copy-done.2) | copy-start | bytes 4718596
  444.0 587.5 %reduce-scatter.16.cloned.1.call-start = ((), (), s32[]{:S(2)}) async-start(), calls=%async_computation.18 | async-start | bytes 1253376 | tf_op jit(solution)/shard_map/reduce_scatter | solution.py:237
  (38 other events, 224.5 us)
Sparse Core Ops, SparseCore 0:
  9.6 12.4 all-gather.7
  24.8 60.2 all-gather.9
  115.4 9.6 reduce-scatter.7
  128.1 63.4 all-gather.13
  193.7 8.6 all-gather.11
  205.3 63.4 all-gather.15
  275.9 9.7 reduce-scatter.9
  291.5 10.9 all-gather.17
  319.6 12.0 reduce-scatter.11
  338.1 10.9 all-gather.19
  420.3 10.2 reduce-scatter.13
  436.1 182.1 all-reduce.4
  624.9 136.2 reduce-scatter.19
  766.8 136.0 reduce-scatter.17
  908.8 122.6 reduce-scatter.15
where the time goes:
time: 1050 us; the launch traced here: 1040 us
  waiting for transfers between devices  658 us (63%)
  blocking collectives  169 us (16%)
  matrix products  138 us (13%)
  other arithmetic  39.6 us (4%)
  between operations  16.1 us (2%)
  local copies, waits for them, and re-layouts  15.8 us (2%)
    reduce_scatter x1, waiting for transfers between devices, per_device(): lax.psum_scatter(up_weight_grad, 'dp', scatter_dimension=0, tiled=True)  142 us
    reduce_scatter x1, waiting for transfers between devices, per_device(): lax.psum_scatter(down_weight_grad, 'dp', scatter_dimension=1, tiled=True)  141 us
    reduce_scatter x1, waiting for transfers between devices, per_device(): lax.psum_scatter(out_weight_grad, 'dp', scatter_dimension=1, tiled=True)  129 us
    psum x1, blocking collectives, per_device(): qv_bias_total, up_bias_total = lax.psum((qv_bias_grad, up_bias_grad), 'dp')  76.4 us
    all_gather x1, waiting for transfers between devices, per_device(): lax.all_gather(up_weight, 'dp', axis=0, tiled=True)  62.5 us
    all_gather x1, blocking collectives, per_device(): lax.all_gather(out_weight, 'dp', axis=1, tiled=True)  49.1 us
    unnamed x16, waiting for transfers between devices  48.2 us
    all_gather x1, waiting for transfers between devices, per_device(): lax.all_gather(down_weight, 'dp', axis=1, tiled=True)  46.7 us
  transfers between devices with their start and end apart: 15, of which 13 were waited for; matrix products, arithmetic and copies ran while one was open for 5% of the time, Pallas kernels for 0%

commit v1 on v0

--- a/solution.py
+++ b/solution.py
@@ -7,6 +7,18 @@
 LENGTH = 1024
 EPSILON = 1e-05
 NEGATIVE = -1e30
+
+
+def collect(array, axis, dim):
+    ways, here, lap = (lax.axis_size(axis), lax.axis_index(axis), array.shape[dim])
+    line, have = (array, 1)
+    while have < ways:
+        line = jnp.concatenate(
+            [line, lax.ppermute(line, axis, [(d, (d - have) % ways) for d in range(ways)])],
+            axis=dim,
+        )
+        have = 2 * have
+    return jnp.roll(line, here * lap, axis=dim)
 
 
 def layer_norm(values, norm_gain, norm_shift):
@@ -60,7 +72,7 @@
     scaling = HEAD_DIM ** (-0.5)
     positions = jnp.arange(LENGTH)
     qkv_full, out_full, up_full, down_full = (
-        lax.all_gather(qkv_weight, "dp", axis=1, tiled=True),
+        collect(qkv_weight, "dp", 1),
         lax.all_gather(out_weight, "dp", axis=1, tiled=True),
         lax.all_gather(up_weight, "dp", axis=0, tiled=True),
         lax.all_gather(down_weight, "dp", axis=1, tiled=True),

time: 1050 us -> 948 us (0.903)
  waiting for transfers between devices: 658 us -> 522 us
  blocking collectives: 169 us -> 183 us
    reduce_scatter x1, waiting for transfers between devices: 141 us -> 8.55 us  [per_device(): lax.psum_scatter(down_weight_grad, 'dp', scatter_dimension=1, tiled=True)]
    all_gather x1 -> x0, waiting for transfers between devices: 25.9 us -> none  [per_device(): lax.all_gather(qkv_weight, 'dp', axis=1, tiled=True)]
    ppermute x0 -> x4, waiting for transfers between devices: none -> 17.1 us  [collect(): lax.ppermute(line, axis, [(d, (d - have) % ways) for d in range(ways)])]
    all_gather x1, blocking collectives: 49.1 us -> 62.3 us  [per_device(): lax.all_gather(out_weight, 'dp', axis=1, tiled=True)]
    all_gather x1, waiting for transfers between devices: 62.5 us -> 51.2 us  [per_device(): lax.all_gather(up_weight, 'dp', axis=0, tiled=True)]
    unnamed x16 -> x15, waiting for transfers between devices: 48.2 us -> 56 us
  transfers between devices with their start and end apart: 15 -> 18, of which waited for: 13 -> 15; matrix products, arithmetic and copies ran while one was open for 5% -> 6% of each run, Pallas kernels for 0% -> 0%
where the time goes in v1:
time: 948 us; the launch traced here: 939 us
  waiting for transfers between devices  522 us (55%)
  blocking collectives  183 us (19%)
  matrix products  139 us (15%)
  other arithmetic  43.7 us (5%)
  local copies, waits for them, and re-layouts  23.1 us (2%)
  between operations  18 us (2%)
  starting transfers between devices  10 us (1%)
    reduce_scatter x1, waiting for transfers between devices, per_device(): lax.psum_scatter(up_weight_grad, 'dp', scatter_dimension=0, tiled=True)  142 us
    reduce_scatter x1, waiting for transfers between devices, per_device(): lax.psum_scatter(out_weight_grad, 'dp', scatter_dimension=1, tiled=True)  129 us
    psum x1, blocking collectives, per_device(): qv_bias_total, up_bias_total = lax.psum((qv_bias_grad, up_bias_grad), 'dp')  76.6 us
    all_gather x1, blocking collectives, per_device(): lax.all_gather(out_weight, 'dp', axis=1, tiled=True)  62.3 us
    unnamed x15, waiting for transfers between devices  56 us
    all_gather x1, waiting for transfers between devices, per_device(): lax.all_gather(up_weight, 'dp', axis=0, tiled=True)  51.2 us
    all_gather x1, waiting for transfers between devices, per_device(): lax.all_gather(down_weight, 'dp', axis=1, tiled=True)  46.7 us
    psum x1, blocking collectives, per_device(): lax.psum((out_bias_grad, down_bias_grad, gain_one_grad, shift_one_grad, g...  43.9 us
  transfers between devices with their start and end apart: 18, of which 15 were waited for; matrix products, arithmetic and copies ran while one was open for 6% of the time, Pallas kernels for 0%

profile of v1, /device:TPU:0, one launch (start us, length us, event | category | flops | bytes accessed | tf_op | source)
XLA Modules:
  0.0 938.8 jit_solution(16854281557498533310)
XLA Ops:
  8.1 7.0 collective-permute-start
  26.5 9.6 %collective-permute-done.2 = bf16[3,192,384]{2,1,0:T(8,128)(2,1)S(1)} collective-permute-done((bf16[3,192,384]{2,1,0:T(8,128)(2,1)S(1)}, bf16[3,192,384]{2,1,0:T(8,128)(2,1)S(1)}, u32[]{:S(2)}, u32[]{:S(2)}) %collective-permute-start.2) | collective-permute-done | bytes 442400 | tf_op jit(solution)/shard_map/ppermute | solution.py:17
  38.6 62.3 %all_gather.22 = bf16[384,768]{0,1:T(8,128)(2,1)} all-gather(bf16[384,48]{0,1:T(8,128)(2,1)S(1)} %copy-done.28), channel_id=1, replica_groups=mesh['dp'=16,'tensor'=2] {'dp'}, dimensions={1}, use_global_device_ids=true | all-gather | bytes 626688 | tf_op jit(solution)/shard_map/all_gather | solution.py:76
  139.0 18.9 %reduce-scatter.8.cloned.1.call-done = f32[512,768]{1,0:T(8,128)} async-done(((f32[1024,768]{1,0:T(8,128)}), f32[512,768]{1,0:T(8,128)}) %reduce-scatter.8.cloned.1.call-update) | async-done | bytes 1572880 | tf_op jit(solution)/shard_map/reduce_scatter | solution.py:123
  161.9 51.2 %all-gather.11.cloned.1.call-done = bf16[768,1536]{1,0:T(8,128)(2,1)} async-done(((bf16[48,1536]{1,0:T(8,128)(2,1)}), bf16[768,1536]{1,0:T(8,128)(2,1)}) %all-gather.11.cloned.1.call-update) | async-done | bytes 2359312 | tf_op jit(solution)/shard_map/all_gather | solution.py:77
  213.1 10.0 %all-gather.9.cloned.1.call-done = bf16[1024,768]{1,0:T(8,128)(2,1)} async-done(((bf16[512,768]{1,0:T(8,128)(2,1)}), bf16[1024,768]{1,0:T(8,128)(2,1)}) %all-gather.9.cloned.1.call-update) | async-done | bytes 1572880 | tf_op jit(solution)/shard_map/all_gather | solution.py:129
  223.2 20.1 %multiply_convert_fusion.2 = (bf16[1024,1536]{1,0:T(8,128)(2,1)}, f32[1024,1536]{1,0:T(8,128)}, f32[1024,1536]{1,0:T(8,128)}) fusion(f32[1536]{0:T(1024)S(1)} %copy-done.45, bf16[1024,768]{1,0:T(8,128)(2,1)} %all-gather.9.cloned.1.call-done, bf16[768,1536]{1,0:T(8,128)(2,1)} %all-gather.11.cloned.1.call-done), kind=kOutput, calls=%fused_computation.24 | convolution fusion | flops 2519728128 | bytes 19666944 | tf_op jit(solution)/shard_map/dot_general | solution.py:35
  243.2 46.7 %all-gather.13.cloned.1.call-done = bf16[1536,768]{0,1:T(8,128)(2,1)} async-done(((bf16[1536,48]{0,1:T(8,128)(2,1)}), bf16[1536,768]{0,1:T(8,128)(2,1)}) %all-gather.13.cloned.1.call-update) | async-done | bytes 2359312 | tf_op jit(solution)/shard_map/all_gather | solution.py:78
  290.0 6.9 fusion.65
  297.0 9.2 reduce-scatter.10.cloned.1.call-done
  313.4 10.7 %all-gather.15.cloned.1.call-done = bf16[1024,768]{1,0:T(8,128)(2,1)} async-done(((bf16[512,768]{1,0:T(8,128)(2,1)}), bf16[1024,768]{1,0:T(8,128)(2,1)}) %all-gather.15.cloned.1.call-update) | async-done | bytes 1572880 | tf_op jit(solution)/shard_map/all_gather | solution.py:144
  324.1 10.9 %convert_reduce_fusion = (f32[1536]{0:T(1024)}, bf16[1024,1536]{1,0:T(8,128)(2,1)S(1)}) fusion(f32[1024,1536]{1,0:T(8,128)} %get-tuple-element.135, f32[1024,1536]{1,0:T(8,128)} %get-tuple-element.146, f32[1536]{0:T(1024)S(1)} %copy-done.45, bf16[1024,768]{1,0:T(8,128)(2,1)} %all-gather.15.cloned.1.call-done, ...), kind=kOutput, calls=%fused_computation.20 | convolution fusion | flops 2442656256 | bytes 19673088 | tf_op jit(solution)/shard_map/dot_general | solution.py:45
  341.1 12.0 %reduce-scatter.12.cloned.1.call-done = f32[512,768]{1,0:T(8,128)} async-done(((f32[1024,768]{1,0:T(8,128)}), f32[512,768]{1,0:T(8,128)}) %reduce-scatter.12.cloned.1.call-update) | async-done | bytes 1572880 | tf_op jit(solution)/shard_map/reduce_scatter | solution.py:152
  359.5 11.1 %all-gather.17.cloned.1.call-done = bf16[1024,768]{1,0:T(8,128)(2,1)} async-done(((bf16[512,768]{1,0:T(8,128)(2,1)}), bf16[1024,768]{1,0:T(8,128)(2,1)}) %all-gather.17.cloned.1.call-update) | async-done | bytes 1572880 | tf_op jit(solution)/shard_map/all_gather | solution.py:159
  373.0 6.4 fusion.67
  379.4 7.7 fusion.5
  387.1 19.0 %multiply_reduce_fusion.1 = (f32[6,512]{1,0:T(8,128)S(1)}, f32[6,512]{1,0:T(8,128)S(1)}, f32[6,512,1024]{2,1,0:T(8,128)}) fusion(f32[6,512]{1,0:T(8,128)S(1)} %get-tuple-element.151, f32[6,512,1024]{2,1,0:T(8,128)} %copy-done.1, pred[1024]{0:T(1024)(128)(4,1)S(1)} %iota_compare_fusion, f32[6,512,1024]{2,1,0:T(8,128)} %fusion.67, ...), kind=kOutput, calls=%fused_computation.4 | convolution fusion | flops 434104320 | bytes 51561472 | tf_op jit(solution)/shard_map/while/body/eval_jaxpr/qhd,khd->hqk/dot_general | solution.py:187
  406.1 17.3 %multiply_convert_fusion.1 = (bf16[6,512,1024]{2,1,0:T(8,128)(2,1)S(1)}, bf16[6,512,1024]{2,1,0:T(8,128)(2,1)S(1)}) fusion(f32[6,512,1024]{2,1,0:T(8,128)} %get-tuple-element.147, f32[6,512]{1,0:T(8,128)S(1)} %get-tuple-element.107, f32[6,512]{1,0:T(8,128)S(1)} %get-tuple-element.151, f32[6,512,1024]{2,1,0:T(8,128)} %copy-done.1, ...), kind=kLoop, calls=%fused_computation.3 | loop fusion | flops 37748736 | bytes 62964736 | tf_op jit(solution)/shard_map/while/body/eval_jaxpr/convert_element_type | solution.py:191
  472.3 43.9 %all-reduce.1 = (f32[768]{0:T(1024)}, f32[768]{0:T(1024)}, f32[768]{0:T(1024)}, f32[768]{0:T(1024)}, f32[768]{0:T(1024)}, /*index=5*/f32[768]{0:T(1024)}) all-reduce(f32[768]{0:T(1024)S(1)} %copy-done.30, f32[768]{0:T(1024)S(1)} %get-tuple-element.121, f32[768]{0:T(1024)S(1)} %copy-done.32, ...), channel_id=1, replica_groups=mesh['dp'=16,'tensor'=2] {'dp','tensor'}, use_global_device_ids=true, to_apply=%region_24.25 | all-reduce | flops 4608 | bytes 36864 | tf_op jit(solution)/shard_map/psum | solution.py:261
  516.5 76.6 %all-reduce.2 = (f32[2,384]{1,0:T(2,128)}, f32[1536]{0:T(1024)}) all-reduce(f32[2,384]{1,0:T(2,128)S(1)} %pad_maximum_fusion.10, f32[1536]{0:T(1024)S(1)} %copy-done.34), channel_id=1, replica_groups=mesh['dp'=16,'tensor'=2] {'dp'}, use_global_device_ids=true, to_apply=%region_21.22 | all-reduce | flops 2304 | bytes 18432 | tf_op jit(solution)/shard_map/psum | solution.py:253
  595.4 54.9 %all-reduce.5.cloned.1.call-done = f32[3,768,384]{2,0,1:T(4,128)} async-done(((f32[3,768,384]{2,0,1:T(4,128)}), f32[3,768,384]{2,0,1:T(4,128)}) %all-reduce.5.cloned.1.call-update) | async-done | bytes 3538960
  652.0 8.6 reduce-scatter.20.cloned.1.call-done
  660.6 141.8 %reduce-scatter.18.cloned.1.call-done = f32[48,1536]{1,0:T(8,128)} async-done(((f32[768,1536]{1,0:T(8,128)}), f32[48,1536]{1,0:T(8,128)}) %reduce-scatter.18.cloned.1.call-update) | async-done | bytes 294928 | tf_op jit(solution)/shard_map/reduce_scatter | solution.py:250
  802.4 128.8 %reduce-scatter.16.cloned.1.call-done = f32[384,48]{0,1:T(8,128)} async-done(((f32[384,768]{0,1:T(8,128)}), f32[384,48]{0,1:T(8,128)}) %reduce-scatter.16.cloned.1.call-update) | async-done | bytes 73744 | tf_op jit(solution)/shard_map/reduce_scatter | solution.py:249
  (211 shorter events, 129.0 us)
Async XLA Ops:
  8.0 100.0 %all-gather.7.cloned.1.call-start = ((), (), s32[]{:S(2)}) async-start(), calls=%async_computation.7 | async-start | bytes 2359296 | tf_op jit(solution)/shard_map/all_gather | solution.py:80
  8.1 9.6 %collective-permute-start = (bf16[3,48,384]{2,1,0:T(8,128)(2,1)}, bf16[3,48,384]{2,1,0:T(8,128)(2,1)S(1)}, u32[]{:S(2)}, u32[]{:S(2)}) collective-permute-start(bf16[3,48,384]{2,1,0:T(8,128)(2,1)} %param.17), channel_id=1, source_target_pairs={{0,30},{2,0},{4,2},{6,4},{8,6},{10,8},{12,10},{14,12},{16,14},{18,... | collective-permute-start | bytes 331784 | tf_op jit(solution)/shard_map/ppermute | solution.py:17
  18.6 6.4 collective-permute-start.1
  26.0 10.2 %collective-permute-start.2 = (bf16[3,192,384]{2,1,0:T(8,128)(2,1)S(1)}, bf16[3,192,384]{2,1,0:T(8,128)(2,1)S(1)}, u32[]{:S(2)}, u32[]{:S(2)}) collective-permute-start(bf16[3,192,384]{2,1,0:T(8,128)(2,1)S(1)} %pad_maximum_fusion.6), channel_id=1, source_target_pairs={{0,24},{2,26},{4,28},{6,30},{8,0},{10,2},{12,4},{14,6},{16,8},{18,... | collective-permute-start | bytes 1327112 | tf_op jit(solution)/shard_map/ppermute | solution.py:17
  26.5 131.5 %reduce-scatter.8.cloned.1.call-start = ((), (), s32[]{:S(2)}) async-start(), calls=%async_computation.8 | async-start | bytes 4718592 | tf_op jit(solution)/shard_map/reduce_scatter | solution.py:123
  37.1 66.0 %collective-permute-start.3 = (bf16[3,384,384]{2,1,0:T(8,128)(2,1)S(1)}, bf16[3,384,384]{2,1,0:T(8,128)(2,1)S(1)}, u32[]{:S(2)}, u32[]{:S(2)}) collective-permute-start(bf16[3,384,384]{2,1,0:T(8,128)(2,1)S(1)} %pad_maximum_fusion.1), channel_id=1, source_target_pairs={{0,16},{2,18},{4,20},{6,22},{8,24},{10,26},{12,28},{14,30},{16,0},... | collective-permute-start | bytes 2654216 | tf_op jit(solution)/shard_map/ppermute | solution.py:17
  138.4 74.7 %all-gather.11.cloned.1.call-start = ((), (), s32[]{:S(2)}) async-start(), calls=%async_computation.10 | async-start | bytes 2506752 | tf_op jit(solution)/shard_map/all_gather | solution.py:77
  139.0 84.2 %copy-start.45 = (f32[1536]{0:T(1024)S(1)}, f32[1536]{0:T(1024)}, u32[]{:S(2)}) copy-start(f32[1536]{0:T(1024)} %param.22) | copy-start | bytes 18436
  139.0 84.2 %all-gather.9.cloned.1.call-start = ((), (), s32[]{:S(2)}) async-start(), calls=%async_computation.9 | async-start | bytes 2359296 | tf_op jit(solution)/shard_map/all_gather | solution.py:129
  161.3 128.7 %all-gather.13.cloned.1.call-start = ((), (), s32[]{:S(2)}) async-start(), calls=%async_computation.11 | async-start | bytes 2506752 | tf_op jit(solution)/shard_map/all_gather | solution.py:78
  161.8 144.4 %reduce-scatter.10.cloned.1.call-start = ((), (), s32[]{:S(2)}) async-start(), calls=%async_computation.12 | async-start | bytes 4718592 | tf_op jit(solution)/shard_map/reduce_scatter | solution.py:134
  296.9 27.2 %all-gather.15.cloned.1.call-start = ((), (), s32[]{:S(2)}) async-start(), calls=%async_computation.13 | async-start | bytes 2359296 | tf_op jit(solution)/shard_map/all_gather | solution.py:144
  313.1 40.0 %reduce-scatter.12.cloned.1.call-start = ((), (), s32[]{:S(2)}) async-start(), calls=%async_computation.14 | async-start | bytes 4718592 | tf_op jit(solution)/shard_map/reduce_scatter | solution.py:152
  341.1 29.6 %all-gather.17.cloned.1.call-start = ((), (), s32[]{:S(2)}) async-start(), calls=%async_computation.15 | async-start | bytes 2359296 | tf_op jit(solution)/shard_map/all_gather | solution.py:159
  359.5 233.7 %reduce-scatter.14.cloned.1.call-start = ((), (), s32[]{:S(2)}) async-start(), calls=%async_computation.16 | async-start | bytes 2359296 | tf_op jit(solution)/shard_map/reduce_scatter | solution.py:236
  442.4 207.9 %all-reduce.5.cloned.1.call-start = ((), (), s32[]{:S(2)}) async-start(), calls=%async_computation.20 | async-start | bytes 9437184
  450.7 209.9 %reduce-scatter.20.cloned.1.call-start = ((), (), s32[]{:S(2)}) async-start(), calls=%async_computation.19 | async-start | bytes 5013504 | tf_op jit(solution)/shard_map/reduce_scatter | solution.py:251
  458.5 343.8 %reduce-scatter.18.cloned.1.call-start = ((), (), s32[]{:S(2)}) async-start(), calls=%async_computation.18 | async-start | bytes 5013504 | tf_op jit(solution)/shard_map/reduce_scatter | solution.py:250
  466.3 49.9 %copy-start.11 = (bf16[6,64,512]{2,1,0:T(8,128)(2,1)S(1)}, bf16[6,64,512]{2,1,0:T(8,128)(2,1)}, u32[]{:S(2)}) copy-start(bf16[6,64,512]{2,1,0:T(8,128)(2,1)} %copy-done.10) | copy-start | bytes 1179652
  466.3 49.9 %copy-start.13 = (bf16[6,64,512]{2,1,0:T(8,128)(2,1)S(1)}, bf16[6,64,512]{2,1,0:T(8,128)(2,1)}, u32[]{:S(2)}) copy-start(bf16[6,64,512]{2,1,0:T(8,128)(2,1)} %copy-done.12) | copy-start | bytes 1179652
  466.3 50.0 %copy-start.36 = (f32[6,64]{1,0:T(8,128)S(1)}, f32[6,64]{1,0:T(8,128)}, u32[]{:S(2)}) copy-start(f32[6,64]{1,0:T(8,128)} %get-tuple-element.148) | copy-start | bytes 4612
  466.3 50.1 %copy-start.34 = (f32[1536]{0:T(1024)S(1)}, f32[1536]{0:T(1024)}, u32[]{:S(2)}) copy-start(f32[1536]{0:T(1024)} %get-tuple-element.125) | copy-start | bytes 18436
  466.3 126.8 %copy-start.3 = (f32[512,768]{1,0:T(8,128)S(1)}, f32[512,768]{1,0:T(8,128)}, u32[]{:S(2)}) copy-start(f32[512,768]{1,0:T(8,128)} %copy-done.2) | copy-start | bytes 4718596
  466.4 464.8 %reduce-scatter.16.cloned.1.call-start = ((), (), s32[]{:S(2)}) async-start(), calls=%async_computation.17 | async-start | bytes 1253376 | tf_op jit(solution)/shard_map/reduce_scatter | solution.py:249
  (45 other events, 427.2 us)
Sparse Core Ops, SparseCore 0:
  26.6 14.3 all-gather.6
  138.5 19.4 reduce-scatter.7
  297.0 9.1 reduce-scatter.9
  359.6 11.0 all-gather.16
  442.5 10.2 reduce-scatter.13
  459.2 201.3 reduce-scatter.19
  666.3 136.0 reduce-scatter.17
  808.4 122.7 reduce-scatter.15
Sparse Core Ops, SparseCore 1:
  142.1 71.0 all-gather.10
  215.2 7.9 all-gather.8
  226.2 63.7 all-gather.12
  313.2 10.8 all-gather.14
  341.1 11.9 reduce-scatter.11
  450.7 199.5 all-reduce.4
